TPU v7x, 512 devices: a whole 4x4x16 slice. The times are simulated.
512 devices in a mesh: traj: 32 (over z_hi, y, core), tm: 16 (over z_lo, x).
Axes of the slice: x: 4, y: 4, z: 16 (z_hi: 4, z_lo: 4; z = z_hi * 4 + z_lo), core: 2. Of those that a mesh axis runs over, the one named last changes fastest.
Arguments:
- states: float32 [16, 32, 8192], P('tm', None, 'traj'), may hold values from -6 to 6
- vectors: bfloat16 [64, 8192], P(None, 'traj'), may hold values from -6 to 6
- kernel_scale: float32 [16], P('tm'), may hold values from 6 to 16
- neighbour_blocks: int32 [64, 24], P('traj'), may hold values from 0 to 63, as said below
- neighbour_count: int32 [64], P('traj'), may hold values from 6 to 24, as said below
Outputs:
- result: float32 [64, 8192], P(None, 'traj')
Inputs may be any that keep to these rules, and one draw needn't show every extreme that they name: `neighbour_blocks`: row b names 24 different blocks, the first of them b itself. Only the first neighbour_count[b] entries of row b of neighbour_blocks are neighbours of block b; some block uses all 24.
All inputs are finite; a program needn't handle non-finite values.
Results may differ from a plain program's by a relative error of at most 0.0013.
Values may be sent and summed in bfloat16 or wider, within the bound.
A program may use at most 64 MiB of HBM per device.

v0:
```python
import math
import jax
import jax.numpy as jnp
from jax import lax
from jax.sharding import Mesh
from jax.sharding import PartitionSpec as P

BLK = 128
TRAJ = ("traj_0", "traj_1", "traj_2")


def in_order(blocks, dim):
    dims = list(blocks.shape[1:])
    dims[dim] *= blocks.shape[0]
    return jnp.moveaxis(blocks, 0, dim).reshape(dims)


def all_blocks(array, axes, turns):
    blocks = array[None]
    for k in turns:
        blocks = lax.all_gather(blocks, axes[k], axis=0, tiled=True)
    block = [lax.axis_size(axes[k]) for k in reversed(turns)]
    blocks = blocks.reshape(*block, *array.shape)
    turned = sorted(range(len(turns)), key=lambda place: turns[len(turns) - 1 - place])
    return blocks.transpose(*turned, *range(len(turns), blocks.ndim)).reshape(-1, *array.shape)


def gather_axes(array, axes, turns, dim):
    return in_order(all_blocks(array, axes, turns), dim)


def sent_together(arrays, axis, dim, along):
    widths = [math.prod(a.shape[along:]) for a in arrays]
    both = jnp.concatenate(
        [a.reshape(*a.shape[:along], w) for a, w in zip(arrays, widths)], axis=along
    )
    out = lax.all_gather(both, axis, axis=dim, tiled=True)
    blocks = jnp.split(out, [sum(widths[:k]) for k in range(1, len(widths))], axis=along)
    return tuple((b.reshape(*out.shape[:along], *a.shape[along:]) for a, b in zip(arrays, blocks)))


def copy_for_each(array, axis):
    copies = jnp.broadcast_to(array, (lax.axis_size(axis), *array.shape))
    return lax.all_to_all(copies, axis, split_axis=0, concat_axis=0, tiled=True)


def of_everyone(array, axis):
    return copy_for_each(array, axis).sum(axis=0)


def linked_blocks(neighbour_blocks, neighbour_count, blocks_total):
    slots = neighbour_blocks.shape[1]
    named = neighbour_blocks[:, :, None] == jnp.arange(blocks_total, dtype=jnp.int32)[None, None, :]
    within = jnp.arange(slots, dtype=jnp.int32)[None, :, None] < neighbour_count[:, None, None]
    return jnp.any(named & within, axis=1).astype(jnp.float32)


def per_device(states, vectors, kernel_scale, neighbour_blocks, neighbour_count):
    coords_all = gather_axes(states, (("traj_0", "traj_1"), "traj_2"), (0, 1), 2)[0]
    vectors_all = lax.all_gather(vectors, TRAJ, axis=1, tiled=True)
    own = states[0]
    spread = kernel_scale[0]
    own_rows = own.shape[1]
    columns = coords_all.shape[1]
    vector_count = vectors.shape[0]
    blocks_total = columns // BLK
    block_rows = own_rows // BLK
    own_squares = jnp.sum(own * own, axis=0)
    all_squares = jnp.sum(coords_all * coords_all, axis=0)
    tile_width = math.gcd(columns, 512)
    tile_count = columns // tile_width
    linked = linked_blocks(neighbour_blocks, neighbour_count, blocks_total)

    def dense_kernel(tile_index):
        offset = tile_index * tile_width
        slab = lax.dynamic_slice_in_dim(coords_all, offset, tile_width, 1)
        cross = lax.dot_general(
            own, slab, (((0,), (0,)), ((), ())), precision=lax.Precision.HIGHEST
        )
        slab_squares = lax.dynamic_slice_in_dim(all_squares, offset, tile_width, 0)
        distance = own_squares[:, None] + slab_squares[None, :] - 2.0 * cross
        mask = lax.dynamic_slice_in_dim(linked, offset // BLK, tile_width // BLK, 1)
        shaped = jnp.exp(-distance / spread).reshape(block_rows, BLK, tile_width // BLK, BLK)
        return (mask[:, None, :, None] * shaped).reshape(own_rows, tile_width)

    def first_dense(tile_index, carry):
        row_sum, pushed = carry
        kernel = dense_kernel(tile_index)
        weights = kernel.astype(jnp.bfloat16)
        slab_vectors = lax.dynamic_slice_in_dim(vectors_all, tile_index * tile_width, tile_width, 1)
        pushed = pushed + lax.dot_general(
            slab_vectors, weights, (((1,), (1,)), ((), ())), preferred_element_type=jnp.float32
        )
        return (row_sum + jnp.sum(kernel, axis=1), pushed)

    row_sum, pushed = lax.fori_loop(
        0,
        tile_count,
        first_dense,
        (jnp.zeros((own_rows,), jnp.float32), jnp.zeros((vector_count, own_rows), jnp.float32)),
    )
    scaled = (pushed / (row_sum * row_sum)[None, :]).astype(jnp.bfloat16)
    lists_whole, counts_whole = sent_together((neighbour_blocks, neighbour_count), TRAJ, 0, 1)
    linked_whole = linked_blocks(lists_whole, counts_whole, blocks_total)
    own_start = lax.axis_index(TRAJ) * block_rows
    column_mask = lax.dynamic_slice_in_dim(linked_whole, own_start, block_rows, 1)
    scaled_whole = lax.all_gather(scaled, TRAJ, axis=1, tiled=True)

    def pull_tile(tile_index, total):
        offset = tile_index * tile_width
        slab = lax.dynamic_slice_in_dim(coords_all, offset, tile_width, 1)
        cross = lax.dot_general(
            slab, own, (((0,), (0,)), ((), ())), precision=lax.Precision.HIGHEST
        )
        slab_squares = lax.dynamic_slice_in_dim(all_squares, offset, tile_width, 0)
        distance = slab_squares[:, None] + own_squares[None, :] - 2.0 * cross
        mask = lax.dynamic_slice_in_dim(column_mask, offset // BLK, tile_width // BLK, 0)
        shaped = jnp.exp(-distance / spread).reshape(tile_width // BLK, BLK, block_rows, BLK)
        weights = (
            (mask[:, None, :, None] * shaped).reshape(tile_width, own_rows).astype(jnp.bfloat16)
        )
        slab_scaled = lax.dynamic_slice_in_dim(scaled_whole, offset, tile_width, 1)
        return total + jnp.dot(slab_scaled, weights, preferred_element_type=jnp.float32)

    own_pulled = lax.fori_loop(
        0, tile_count, pull_tile, jnp.zeros((vector_count, own_rows), jnp.float32)
    )
    result = of_everyone(own_pulled, "tm")
    return result


def solution(mesh):
    split = Mesh(
        mesh.devices.reshape(4, 4, 2, mesh.shape["tm"]), ("traj_0", "traj_1", "traj_2", "tm")
    )
    in_specs = (P("tm", None, TRAJ), P(None, TRAJ), P("tm"), P(TRAJ, None), P(TRAJ))
    out_specs = P(None, TRAJ)
    return jax.shard_map(
        per_device, mesh=split, in_specs=in_specs, out_specs=out_specs, check_vma=False
    )
```

profile of v0, /device:TPU:8, one launch (start us, length us, event | category | flops | bytes accessed | tf_op | source)
XLA Modules:
  0.0 365.6 jit_solution(11835117052081428395)
XLA Ops:
  6.5 60.4 %all-gather = f32[16,32,256]{2,1,0:T(8,128)} all-gather(f32[1,32,256]{2,1,0:T(8,128)} %param.9), channel_id=2, replica_groups=mesh['traj_0'=4,'traj_1'=4,'traj_2'=2,'tm'=16] {'traj_0','traj_1'}, dimensions={0}, use_global_device_ids=true | all-gather | bytes 557056 | tf_op jit(solution)/shard_map/all_gather | solution.py:21
  69.3 16.1 %all-gather.11.cloned.1.call-done = f32[32,32,256]{2,1,0:T(8,128)} async-done(((f32[16,32,256]{2,1,0:T(8,128)}), f32[32,32,256]{2,1,0:T(8,128)}) %all-gather.11.cloned.1.call-update) | async-done | bytes 1048592 | tf_op jit(solution)/shard_map/all_gather | solution.py:21
  85.4 1.3 copy.19
  87.0 74.4 %all-gather.7.cloned.1.call-done = bf16[64,8192]{1,0:T(8,128)(2,1)} async-done(((bf16[64,256]{1,0:T(8,128)(2,1)}), bf16[64,8192]{1,0:T(8,128)(2,1)}) %all-gather.7.cloned.1.call-update) | async-done | bytes 1048592 | tf_op jit(solution)/shard_map/all_gather | solution.py:60
  161.4 47.5 %while.34 = (s32[]{:T(128)}, f32[256]{0:T(256)S(1)}, f32[64,256]{1,0:T(8,128)S(1)}, f32[2,64]{1,0:T(2,128)S(1)}, f32[256]{0:T(256)S(1)}, /*index=5*/f32[8192]{0:...) while((s32[]{:T(128)}, f32[256]{0:T(256)S(1)}, ...), condition=%wide.region_6.7_spmd.clone, body=%wide.region_4.0_spmd.clone.sunk | while | flops 68190488 | bytes 1879617 | solution.py:96
  161.9 1.4 fusion.42
  164.9 1.4 fusion.42
  167.8 1.4 fusion.42
  169.2 1.0 convolution_add_fusion.4
  170.8 1.4 fusion.42
  173.8 1.4 fusion.42
  176.8 1.4 fusion.42
  179.7 1.4 fusion.42
  182.7 1.4 fusion.42
  185.7 1.4 fusion.42
  188.6 1.4 fusion.42
  191.6 1.4 fusion.42
  194.6 1.4 fusion.42
  196.0 1.0 convolution_add_fusion.4
  197.6 1.4 fusion.42
  200.5 1.4 fusion.42
  201.9 1.0 convolution_add_fusion.4
  203.5 1.4 fusion.42
  204.9 1.0 convolution_add_fusion.4
  206.5 1.4 fusion.42
  209.8 47.4 %all-gather.2 = s32[32,2,25]{2,1,0:T(2,128)S(1)} all-gather(s32[1,2,25]{2,1,0:T(2,128)S(1)} %add_bitcast_fusion), channel_id=1, replica_groups=mesh['traj_0'=4,'traj_1'=4,'traj_2'=2,'tm'=16] {'traj_0','traj_1','traj_2'}, dimensions={0}, use_global_device_ids=true | all-gather | bytes 6600 | tf_op jit(solution)/shard_map/all_gather | solution.py:37
  258.1 20.6 %all-gather.9.cloned.1.call-done = bf16[64,8192]{1,0:T(8,128)(2,1)} async-done(((bf16[64,256]{1,0:T(8,128)(2,1)}), bf16[64,8192]{1,0:T(8,128)(2,1)}) %all-gather.9.cloned.1.call-update) | async-done | bytes 1048592 | tf_op jit(solution)/shard_map/all_gather | solution.py:107
  278.7 44.3 %while.35 = (s32[]{:T(128)}, f32[64,256]{1,0:T(8,128)S(1)}, bf16[64,8192]{1,0:T(8,128)(2,1)}, f32[64,2]{1,0:T(8,128)S(1)}, f32[8192]{0:T(1024)S(1)}, /*index=5*/...) while((s32[]{:T(128)}, f32[64,256]{1,0:T(8,128)S(1)}, ...), condition=%wide.region_8.9_spmd.clone, body=%wide.region_7.8_spmd.clone.sunk | while | flops 68059160 | bytes 1875448 | solution.py:125
  279.0 1.4 fusion.47
  281.8 1.4 fusion.47
  284.6 1.4 fusion.47
  287.4 1.4 fusion.47
  290.1 1.4 fusion.47
  291.5 1.0 convolution_add_fusion.5
  292.9 1.4 fusion.47
  295.7 1.4 fusion.47
  298.4 1.4 fusion.47
  299.8 1.0 convolution_add_fusion.5
  301.2 1.4 fusion.47
  304.0 1.4 fusion.47
  306.8 1.4 fusion.47
  308.1 1.0 convolution_add_fusion.5
  309.5 1.4 fusion.47
  312.3 1.4 fusion.47
  315.1 1.4 fusion.47
  317.9 1.4 fusion.47
  320.6 1.4 fusion.47
  323.2 35.2 %all_to_all.5 = f32[16,64,256]{2,1,0:T(8,128)S(1)} all-to-all(f32[16,64,256]{2,1,0:T(8,128)S(1)} %broadcast_in_dim.37), channel_id=1, replica_groups=mesh['traj_0'=4,'traj_1'=4,'traj_2'=2,'tm'=16] {'tm'}, dimensions={0} | all-to-all | bytes 2097152 | tf_op jit(solution)/shard_map/all_to_all | solution.py:44
  (186 shorter events, 42.9 us)
Async XLA Ops:
  6.5 78.9 %all-gather.11.cloned.1.call-start = ((), (), s32[]{:S(2)}) async-start(), calls=%async_computation.3 | async-start | bytes 1572864 | tf_op jit(solution)/shard_map/all_gather | solution.py:21
  67.0 2.3 copy-start
  67.0 94.4 %all-gather.7.cloned.1.call-start = ((), (), s32[]{:S(2)}) async-start(), calls=%async_computation.1 | async-start | bytes 1081344 | tf_op jit(solution)/shard_map/all_gather | solution.py:60
  67.8 211.0 %all-gather.9.cloned.1.call-start = ((), (), s32[]{:S(2)}) async-start(), calls=%async_computation.2 | async-start | bytes 1081344 | tf_op jit(solution)/shard_map/all_gather | solution.py:107
  67.8 0.7 copy-start.2
  68.5 0.7 copy-start.1
Sparse Core Ops, SparseCore 0:
  67.1 18.2 all-gather.10
  88.4 72.9 all-gather.6
  209.7 68.9 all-gather.8
where the time goes:
time: 368 us; the launch traced here: 366 us
  blocking collectives  143 us (39%)
  waiting for transfers between devices  112 us (30%)
  matrix products  77.2 us (21%)
  local copies, waits for them, and re-layouts  15 us (4%)
  between operations  13.3 us (4%)
    all_gather x1, waiting for transfers between devices, per_device(): vectors_all = lax.all_gather(vectors, TRAJ, axis=1, tiled=True)  74.4 us
    all_gather x1, blocking collectives, all_blocks(): blocks = lax.all_gather(blocks, axes[k], axis=0, tiled=True)  60.4 us
    all_gather x1, blocking collectives, sent_together(): out = lax.all_gather(both, axis, axis=dim, tiled=True)  47.4 us
    all_to_all x1, blocking collectives, copy_for_each(): return lax.all_to_all(copies, axis, split_axis=0, concat_axis=0, tiled=True)  35.2 us
    dot_general x16, matrix products, dense_kernel(): lax.dot_general(own, slab, (((0,), (0,)), ((), ())), precision=lax.Precis...  22.3 us
    dot_general x16, matrix products, pull_tile(): lax.dot_general(slab, own, (((0,), (0,)), ((), ())), precision=lax.Precis...  21.9 us
    all_gather x1, waiting for transfers between devices, per_device(): scaled_whole = lax.all_gather(scaled, TRAJ, axis=1, tiled=True)  20.6 us
    dot_general x16, matrix products, first_dense(): lax.dot_general(slab_vectors, weights, (((1,), (1,)), ((), ())), preferre...  16.5 us
  transfers between devices with their start and end apart: 3, of which 3 were waited for; matrix products, arithmetic and copies ran while one was open for 1% of the time, Pallas kernels for 0%

commit v1 on v0

--- a/solution.py
+++ b/solution.py
@@ -18,7 +18,9 @@
 def all_blocks(array, axes, turns):
     blocks = array[None]
     for k in turns:
-        blocks = lax.all_gather(blocks, axes[k], axis=0, tiled=True)
+        blocks = jnp.concatenate(
+            lax.all_to_all(jnp.stack([blocks] * lax.axis_size(axes[k])), axes[k], 0, 0), axis=0
+        )
     block = [lax.axis_size(axes[k]) for k in reversed(turns)]
     blocks = blocks.reshape(*block, *array.shape)
     turned = sorted(range(len(turns)), key=lambda place: turns[len(turns) - 1 - place])

time: 368 us -> 311 us (0.85)
  blocking collectives: 143 us -> 87.3 us
  waiting for transfers between devices: 112 us -> 90.4 us
  starting transfers between devices: 0.08 us -> 18.3 us
    all_gather x1 -> x0, blocking collectives: 60.4 us -> none  [all_blocks(): blocks = lax.all_gather(blocks, axes[k], axis=0, tiled=True)]
    all_gather x1, waiting for transfers between devices: 74.4 us -> 44.6 us  [per_device(): vectors_all = lax.all_gather(vectors, TRAJ, axis=1, tiled=True)]
    all_to_all x0 -> x1, waiting for transfers between devices: none -> 24.6 us  [all_blocks(): lax.all_to_all(jnp.stack([blocks] * lax.axis_size(axes[k])), axes[k], 0, 0)]
    all_to_all x0 -> x1, starting transfers between devices: none -> 18.2 us  [all_blocks(): lax.all_to_all(jnp.stack([blocks] * lax.axis_size(axes[k])), axes[k], 0, 0)]
    all_gather x1 -> x0, waiting for transfers between devices: 16.1 us -> none  [all_blocks(): blocks = lax.all_gather(blocks, axes[k], axis=0, tiled=True)]
    all_to_all x0 -> x1, blocking collectives: none -> 4.58 us  [all_blocks(): lax.all_to_all(jnp.stack([blocks] * lax.axis_size(axes[k])), axes[k], 0, 0)]
where the time goes in v1:
time: 311 us; the launch traced here: 309 us
  waiting for transfers between devices  90.4 us (29%)
  blocking collectives  87.3 us (28%)
  matrix products  77.2 us (25%)
  starting transfers between devices  18.3 us (6%)
  local copies, waits for them, and re-layouts  16.4 us (5%)
  between operations  13.6 us (4%)
    all_gather x1, blocking collectives, sent_together(): out = lax.all_gather(both, axis, axis=dim, tiled=True)  47.5 us
    all_gather x1, waiting for transfers between devices, per_device(): vectors_all = lax.all_gather(vectors, TRAJ, axis=1, tiled=True)  44.6 us
    all_to_all x1, blocking collectives, copy_for_each(): return lax.all_to_all(copies, axis, split_axis=0, concat_axis=0, tiled=True)  35.2 us
    all_to_all x1, waiting for transfers between devices, all_blocks(): lax.all_to_all(jnp.stack([blocks] * lax.axis_size(axes[k])), axes[k], 0, 0)  24.6 us
    dot_general x16, matrix products, dense_kernel(): lax.dot_general(own, slab, (((0,), (0,)), ((), ())), precision=lax.Precis...  22.3 us
    dot_general x16, matrix products, pull_tile(): lax.dot_general(slab, own, (((0,), (0,)), ((), ())), precision=lax.Precis...  21.9 us
    all_gather x1, waiting for transfers between devices, per_device(): scaled_whole = lax.all_gather(scaled, TRAJ, axis=1, tiled=True)  20.6 us
    all_to_all x1, starting transfers between devices, all_blocks(): lax.all_to_all(jnp.stack([blocks] * lax.axis_size(axes[k])), axes[k], 0, 0)  18.2 us
  transfers between devices with their start and end apart: 3, of which 3 were waited for; matrix products, arithmetic and copies ran while one was open for 1% of the time, Pallas kernels for 0%

profile of v1, /device:TPU:8, one launch (start us, length us, event | category | flops | bytes accessed | tf_op | source)
XLA Modules:
  0.0 308.5 jit_solution(9189581458818021711)
XLA Ops:
  6.5 1.6 stack.6
  8.2 18.2 %all-to-all-start = ((f32[16,1,1,32,256]{4,3,2,1,0:T(8,128)}), f32[16,1,1,32,256]{4,3,2,1,0:T(8,128)S(1)}, u32[]{:S(2)}, u32[]{:S(2)}) async-start(f32[16,1,1,32,256]{4,3,2,1,0:T(8,128)} %stack.6), calls=%async_computation | async-start | bytes 1048576 | tf_op jit(solution)/shard_map/all_to_all | solution.py:22
  28.6 24.6 %all-to-all-done = f32[16,1,1,32,256]{4,3,2,1,0:T(8,128)S(1)} async-done(((f32[16,1,1,32,256]{4,3,2,1,0:T(8,128)}), f32[16,1,1,32,256]{4,3,2,1,0:T(8,128)S(1)}, u32[]{:S(2)}, u32[]{:S(2)}) %all-to-all-start) | async-done | bytes 524320 | tf_op jit(solution)/shard_map/all_to_all | solution.py:22
  54.0 4.6 %all_to_all.15 = f32[2,16,1,32,256]{4,1,3,2,0:T(8,128)S(1)} all-to-all(f32[2,16,1,32,256]{4,1,3,2,0:T(8,128)S(1)} %copy.22), channel_id=1, replica_groups=mesh['traj_0'=4,'traj_1'=4,'traj_2'=2,'tm'=16] {'traj_2'}, dimensions={0} | all-to-all | bytes 2097152 | tf_op jit(solution)/shard_map/all_to_all | solution.py:22
  59.4 44.6 %all-gather.4.cloned.1.call-done = bf16[64,8192]{1,0:T(8,128)(2,1)} async-done(((bf16[64,256]{1,0:T(8,128)(2,1)}), bf16[64,8192]{1,0:T(8,128)(2,1)}) %all-gather.4.cloned.1.call-update) | async-done | bytes 1048592 | tf_op jit(solution)/shard_map/all_gather | solution.py:62
  104.0 47.5 %while.34 = (s32[]{:T(128)}, f32[256]{0:T(256)S(1)}, f32[64,256]{1,0:T(8,128)S(1)}, f32[2,64]{1,0:T(2,128)S(1)}, f32[256]{0:T(256)S(1)}, /*index=5*/f32[8192]{0:...) while((s32[]{:T(128)}, f32[256]{0:T(256)S(1)}, ...), condition=%wide.region_6.7_spmd.clone, body=%wide.region_4.0_spmd.clone.sunk | while | flops 68190488 | bytes 1879617 | solution.py:98
  104.5 1.4 fusion.42
  107.4 1.4 fusion.42
  110.4 1.4 fusion.42
  111.8 1.0 convolution_add_fusion.4
  113.4 1.4 fusion.42
  116.4 1.4 fusion.42
  117.8 1.0 convolution_add_fusion.4
  119.3 1.4 fusion.42
  122.3 1.4 fusion.42
  123.7 1.0 convolution_add_fusion.4
  125.3 1.4 fusion.42
  128.2 1.4 fusion.42
  131.2 1.4 fusion.42
  134.2 1.4 fusion.42
  137.1 1.4 fusion.42
  140.1 1.4 fusion.42
  143.1 1.4 fusion.42
  146.0 1.4 fusion.42
  149.0 1.4 fusion.42
  152.3 47.5 %all-gather = s32[32,2,25]{2,1,0:T(2,128)S(1)} all-gather(s32[1,2,25]{2,1,0:T(2,128)S(1)} %add_bitcast_fusion), channel_id=1, replica_groups=mesh['traj_0'=4,'traj_1'=4,'traj_2'=2,'tm'=16] {'traj_0','traj_1','traj_2'}, dimensions={0}, use_global_device_ids=true | all-gather | bytes 6600 | tf_op jit(solution)/shard_map/all_gather | solution.py:39
  200.7 20.6 %all-gather.6.cloned.1.call-done = bf16[64,8192]{1,0:T(8,128)(2,1)} async-done(((bf16[64,256]{1,0:T(8,128)(2,1)}), bf16[64,8192]{1,0:T(8,128)(2,1)}) %all-gather.6.cloned.1.call-update) | async-done | bytes 1048592 | tf_op jit(solution)/shard_map/all_gather | solution.py:109
  221.3 44.3 %while.35 = (s32[]{:T(128)}, f32[64,256]{1,0:T(8,128)S(1)}, bf16[64,8192]{1,0:T(8,128)(2,1)}, f32[64,2]{1,0:T(8,128)S(1)}, f32[8192]{0:T(1024)S(1)}, /*index=5*/...) while((s32[]{:T(128)}, f32[64,256]{1,0:T(8,128)S(1)}, ...), condition=%wide.region_8.9_spmd.clone, body=%wide.region_7.8_spmd.clone.sunk | while | flops 68059160 | bytes 1875448 | solution.py:127
  221.6 1.4 fusion.47
  223.0 1.0 convolution_add_fusion.5
  224.4 1.4 fusion.47
  227.2 1.4 fusion.47
  229.9 1.4 fusion.47
  232.7 1.4 fusion.47
  234.1 1.0 convolution_add_fusion.5
  235.5 1.4 fusion.47
  238.3 1.4 fusion.47
  241.0 1.4 fusion.47
  243.8 1.4 fusion.47
  246.6 1.4 fusion.47
  249.4 1.4 fusion.47
  250.7 1.0 convolution_add_fusion.5
  252.1 1.4 fusion.47
  254.9 1.4 fusion.47
  257.7 1.4 fusion.47
  260.5 1.4 fusion.47
  263.2 1.4 fusion.47
  265.8 35.2 %all_to_all.16 = f32[16,64,256]{2,1,0:T(8,128)S(1)} all-to-all(f32[16,64,256]{2,1,0:T(8,128)S(1)} %broadcast_in_dim.33), channel_id=1, replica_groups=mesh['traj_0'=4,'traj_1'=4,'traj_2'=2,'tm'=16] {'tm'}, dimensions={0} | all-to-all | bytes 2097152 | tf_op jit(solution)/shard_map/all_to_all | solution.py:46
  (188 shorter events, 45.2 us)
Async XLA Ops:
  8.2 45.1 %all-to-all-start = ((f32[16,1,1,32,256]{4,3,2,1,0:T(8,128)}), f32[16,1,1,32,256]{4,3,2,1,0:T(8,128)S(1)}, u32[]{:S(2)}, u32[]{:S(2)}) async-start(f32[16,1,1,32,256]{4,3,2,1,0:T(8,128)} %stack.6), calls=%async_computation | async-start | bytes 1048576 | tf_op jit(solution)/shard_map/all_to_all | solution.py:22
  26.3 2.2 copy-start
  26.4 77.7 %all-gather.4.cloned.1.call-start = ((), (), s32[]{:S(2)}) async-start(), calls=%async_computation.3 | async-start | bytes 1081344 | tf_op jit(solution)/shard_map/all_gather | solution.py:62
  27.1 194.2 %all-gather.6.cloned.1.call-start = ((), (), s32[]{:S(2)}) async-start(), calls=%async_computation.4 | async-start | bytes 1081344 | tf_op jit(solution)/shard_map/all_gather | solution.py:109
  27.1 0.7 copy-start.2
  27.8 0.7 copy-start.1
Sparse Core Ops, SparseCore 0:
  30.2 73.7 all-gather.3
  152.3 69.0 all-gather.5
